TPU v7x, 32 devices: a whole 2x2x4 slice. The times are simulated.
32 devices in a mesh: groups: 2 (over y), rows: 4 (over z), shard: 4 (over x, core).
Axes of the slice: x: 2, y: 2, z: 4, core: 2. Of those that a mesh axis runs over, the one named last changes fastest.
Arguments:
- images: bfloat16 [8, 8, 128, 512], P(('groups', 'shard'), 'rows'), parts along dimension 0, may hold values from -6 to 6
- cotangent: bfloat16 [8, 8, 128, 512], P(('groups', 'shard'), 'rows'), parts along dimension 0, may hold values from -6 to 6
- weight_in: bfloat16 [2, 512, 512], P(None, 'shard'), may hold values from -0.25 to 0.25
- weight_group: bfloat16 [2, 144, 512], P(None, 'shard'), may hold values from -0.5 to 0.5
- weight_out: bfloat16 [2, 512, 512], P(None, 'shard'), may hold values from -0.25 to 0.25
Outputs:
- decoded: bfloat16 [8, 8, 128, 512], P(('groups', 'shard'), 'rows'), parts along dimension 0
- grad_images: bfloat16 [8, 8, 128, 512], P(('groups', 'shard'), 'rows'), parts along dimension 0
- grad_in: float32 [4, 512, 512], P('groups', 'shard'), parts along dimension 0
- grad_group: float32 [4, 144, 512], P('groups', 'shard'), parts along dimension 0
- grad_out: float32 [4, 512, 512], P('groups', 'shard'), parts along dimension 0
There are 2 independent parts, one for each index of `groups`. A program takes and returns all parts, laid end to end along the dimension named above; an argument that names none is the same for every part. Nothing has to cross between parts.
All inputs are finite; a program needn't handle non-finite values.
Results may differ from a plain program's by a relative error of at most 0.02.
Values may be sent and summed in bfloat16 or wider, within the bound.
A program may use at most 128 MiB of HBM per device.

v0:
```python
import math
import jax
import jax.numpy as jnp
from jax import lax
from jax.sharding import PartitionSpec as P

GW = 16


def extended_2(cells, sides, width):
    for axis, dim in sides:
        count = lax.axis_size(axis)
        ends = count - 1
        head = lax.slice_in_dim(cells, 0, width, axis=dim)
        tail = lax.slice_in_dim(cells, cells.shape[dim] - width, cells.shape[dim], axis=dim)
        cells = jnp.concatenate(
            [
                lax.ppermute(tail, axis, [(i, (i + 1) % count) for i in range(ends)]),
                cells,
                lax.ppermute(head, axis, [((i + 1) % count, i) for i in range(ends)]),
            ],
            axis=dim,
        )
    return cells


def silu_slope(preact):
    sigmoid_value = jax.nn.sigmoid(preact)
    return sigmoid_value * (1.0 + preact * (1.0 - sigmoid_value))


def block_kernel(full_group, hidden_width, group_width):
    sub_width = min(hidden_width, 128)
    sections = hidden_width // sub_width
    members = sub_width // group_width
    arranged = full_group.reshape(9, group_width, sections, members, group_width)
    arranged = arranged.transpose(0, 2, 3, 1, 4)
    identity = jnp.eye(members, dtype=full_group.dtype)
    expanded = arranged[:, :, :, :, None, :] * identity[None, None, :, None, :, None]
    return expanded.reshape(9, sections, sub_width, sub_width)


def grouped_taps(padded, kernel, out_rows, out_cols, flipped, pattern):
    summed = None
    for tap_index in range(9):
        row_step = tap_index // 3
        col_step = tap_index % 3
        if flipped:
            row_step = 2 - row_step
            col_step = 2 - col_step
        window = padded[:, row_step : row_step + out_rows, col_step : col_step + out_cols, :]
        window = window.reshape(-1, kernel.shape[1], kernel.shape[2])
        tap_term = jnp.einsum(
            pattern, window, kernel[tap_index], preferred_element_type=jnp.float32
        )
        summed = tap_term if summed is None else summed + tap_term
    return summed


def body(images, cotangent, weight_in, weight_group, weight_out):
    tile_count, height, across, channels = images.shape
    block_count = weight_in.shape[0]
    group_width = GW
    pixels = tile_count * height * across
    current = images.reshape(pixels, channels)
    stored = []
    for block_index in range(block_count):
        full_in, full_group, full_out = (
            lax.all_gather(weight_in[block_index], "shard", axis=0, tiled=True),
            lax.all_gather(weight_group[block_index], "shard", axis=0, tiled=True),
            lax.all_gather(weight_out[block_index], "shard", axis=0, tiled=True),
        )
        hidden_width = full_in.shape[1]
        kernel = block_kernel(full_group, hidden_width, group_width)
        pre_one = jnp.dot(current, full_in, preferred_element_type=jnp.float32)
        hidden_one = (
            jax.nn.silu(pre_one)
            .astype(jnp.bfloat16)
            .reshape(tile_count, height, across, hidden_width)
        )
        haloed = extended_2(hidden_one, (("rows", 1),), 1)
        padded_one = jnp.pad(haloed, ((0, 0), (0, 0), (1, 1), (0, 0)))
        pre_two = grouped_taps(padded_one, kernel, height, across, False, "psi,sio->pso").reshape(
            pixels, hidden_width
        )
        hidden_two = jax.nn.silu(pre_two).astype(jnp.bfloat16)
        pre_three = current.astype(jnp.float32) + jnp.dot(
            hidden_two, full_out, preferred_element_type=jnp.float32
        )
        kept_weights = None
        stored.append((current, pre_one, padded_one, pre_two, hidden_two, pre_three, kept_weights))
        current = jax.nn.silu(pre_three).astype(jnp.bfloat16)
    decoded = current.reshape(images.shape)
    grad_flow = cotangent.reshape(pixels, channels)
    shares = []
    for block_index in reversed(range(block_count)):
        flow_in, pre_one, padded_one, pre_two, hidden_two, pre_three, kept_weights = stored[
            block_index
        ]
        full_in, full_group, full_out = (
            lax.all_gather(weight_in[block_index], "shard", axis=0, tiled=True),
            lax.all_gather(weight_group[block_index], "shard", axis=0, tiled=True),
            lax.all_gather(weight_out[block_index], "shard", axis=0, tiled=True),
        )
        hidden_width = full_in.shape[1]
        kernel = block_kernel(full_group, hidden_width, group_width)
        sections = kernel.shape[1]
        sub_width = kernel.shape[2]
        members = sub_width // group_width
        slope_three = grad_flow.astype(jnp.float32) * silu_slope(pre_three)
        low_three = slope_three.astype(jnp.bfloat16)
        part_out = jnp.einsum(
            "pw,pc->wc", hidden_two, low_three, preferred_element_type=jnp.float32
        )
        slope_two = (
            jnp.einsum("pc,wc->pw", low_three, full_out, preferred_element_type=jnp.float32)
            * silu_slope(pre_two)
        ).astype(jnp.bfloat16)
        slope_sections = slope_two.reshape(pixels, sections, sub_width)
        tap_terms = []
        for tap_index in range(9):
            row_step = tap_index // 3
            col_step = tap_index % 3
            window = padded_one[:, row_step : row_step + height, col_step : col_step + across, :]
            window = window.reshape(pixels, sections, sub_width)
            blockwise = jnp.einsum(
                "psi,pso->sio", window, slope_sections, preferred_element_type=jnp.float32
            )
            blockwise = blockwise.reshape(sections, members, group_width, members, group_width)
            same = jnp.eye(members, dtype=jnp.float32)[None, :, None, :, None]
            diagonal_part = jnp.sum(blockwise * same, axis=1)
            tap_terms.append(diagonal_part.transpose(1, 0, 2, 3).reshape(group_width, hidden_width))
        part_group = jnp.stack(tap_terms).reshape(9 * group_width, hidden_width)
        slope_grid = slope_two.reshape(tile_count, height, across, hidden_width)
        padded_slope = jnp.pad(slope_grid, ((0, 0), (2, 2), (1, 1), (0, 0)))
        extended = grouped_taps(padded_slope, kernel, height + 2, across, True, "pso,sio->psi")
        extended = extended.reshape(tile_count, height + 2, across, hidden_width)
        edge_rows = jnp.concatenate([extended[:, :1], extended[:, -1:]], axis=1)
        borders = extended_2(edge_rows.astype(jnp.bfloat16), (("rows", 1),), 1).astype(
            edge_rows.dtype
        )
        back_one = extended[:, 1:-1]
        back_one = back_one.at[:, :1].add(borders[:, :1])
        back_one = back_one.at[:, -1:].add(borders[:, -1:])
        slope_one = (back_one.reshape(pixels, hidden_width) * silu_slope(pre_one)).astype(
            jnp.bfloat16
        )
        part_in = jnp.einsum("pc,pw->cw", flow_in, slope_one, preferred_element_type=jnp.float32)
        grad_flow = (
            slope_three
            + jnp.einsum("pw,cw->pc", slope_one, full_in, preferred_element_type=jnp.float32)
        ).astype(jnp.bfloat16)
        shares.append(
            (
                lax.psum_scatter(
                    part_in.astype(jnp.bfloat16), "shard", scatter_dimension=0, tiled=True
                ).astype(jnp.float32),
                lax.psum_scatter(
                    part_group.astype(jnp.bfloat16), "shard", scatter_dimension=0, tiled=True
                ).astype(jnp.float32),
                lax.psum_scatter(
                    part_out.astype(jnp.bfloat16), "shard", scatter_dimension=0, tiled=True
                ).astype(jnp.float32),
            )
        )
    shares = shares[::-1]
    totals = (
        lax.psum(jnp.stack([entry[0] for entry in shares]).astype(jnp.bfloat16), "rows").astype(
            jnp.float32
        ),
        lax.psum(jnp.stack([entry[1] for entry in shares]).astype(jnp.bfloat16), "rows").astype(
            jnp.float32
        ),
        lax.psum(jnp.stack([entry[2] for entry in shares]).astype(jnp.bfloat16), "rows").astype(
            jnp.float32
        ),
    )
    norm_factor = 1.0 / math.sqrt(pixels * lax.axis_size("rows") * lax.axis_size("shard"))
    grad_images = grad_flow.reshape(images.shape)
    return (
        decoded,
        grad_images,
        totals[0] * norm_factor,
        totals[1] * norm_factor,
        totals[2] * norm_factor,
    )


def solution(mesh):
    placed = (
        P(("groups", "shard"), "rows", None, None),
        P(("groups", "shard"), "rows", None, None),
        P(None, "shard", None),
        P(None, "shard", None),
        P(None, "shard", None),
    )
    return jax.shard_map(
        body,
        mesh=mesh,
        in_specs=placed,
        out_specs=(
            P(("groups", "shard"), "rows", None, None),
            P(("groups", "shard"), "rows", None, None),
            P("groups", "shard", None),
            P("groups", "shard", None),
            P("groups", "shard", None),
        ),
        check_vma=False,
    )
```

profile of v0, /device:TPU:0, one launch (start us, length us, event | category | flops | bytes accessed | tf_op | source)
XLA Modules:
  0.0 473.4 jit_solution(3516267203745144367)
XLA Ops:
  8.9 8.6 %all-gather.1 = bf16[1,512,512]{2,1,0:T(8,128)(2,1)S(1)} all-gather(bf16[1,128,512]{2,1,0:T(8,128)(2,1)S(1)} %get-tuple-element.160), channel_id=3, replica_groups=mesh['groups'=2,'rows'=4,'shard'=4] {'shard'}, dimensions={1}, use_global_device_ids=true | all-gather | bytes 655360 | tf_op jit(solution)/shard_map/all_gather | solution.py:69
  18.3 2.1 multiply_convert_fusion.5
  22.4 5.2 %collective-permute-start = (bf16[1,1,128,512]{3,2,1,0:T(8,128)(2,1)}, bf16[1,1,128,512]{3,2,1,0:T(8,128)(2,1)}, u32[]{:S(2)}, u32[]{:S(2)}) collective-permute-start(bf16[1,1,128,512]{3,2,1,0:T(8,128)(2,1)} %get-tuple-element.158), channel_id=1, source_target_pairs={{0,4},{4,8},{8,12},{1,5},{5,9},{9,13},{2,6},{6,10},{10,14},{3,7},{... | collective-permute-start | bytes 393224 | tf_op jit(solution)/shard_map/ppermute | solution.py:18
  29.4 5.9 %all-gather = bf16[1,144,512]{2,0,1:T(2,128)(2,1)S(1)} all-gather(bf16[1,36,512]{2,0,1:T(2,128)(2,1)S(1)} %get-tuple-element.164), channel_id=2, replica_groups=mesh['groups'=2,'rows'=4,'shard'=4] {'shard'}, dimensions={1}, use_global_device_ids=true | all-gather | bytes 184320 | tf_op jit(solution)/shard_map/all_gather | solution.py:70
  38.4 6.0 %all-gather.3 = bf16[1,144,512]{2,0,1:T(2,128)(2,1)S(1)} all-gather(bf16[1,36,512]{2,0,1:T(2,128)(2,1)S(1)} %get-tuple-element.165), channel_id=5, replica_groups=mesh['groups'=2,'rows'=4,'shard'=4] {'shard'}, dimensions={1}, use_global_device_ids=true | all-gather | bytes 184320 | tf_op jit(solution)/shard_map/all_gather | solution.py:70
  47.7 9.4 %all-gather.4 = bf16[1,512,512]{2,1,0:T(8,128)(2,1)} all-gather(bf16[1,128,512]{2,1,0:T(8,128)(2,1)} %get-tuple-element.161), channel_id=6, replica_groups=mesh['groups'=2,'rows'=4,'shard'=4] {'shard'}, dimensions={1}, use_global_device_ids=true | all-gather | bytes 655360 | tf_op jit(solution)/shard_map/all_gather | solution.py:69
  57.0 4.3 broadcast_multiply_fusion.1
  61.4 8.6 %fusion.110 = (bf16[1,4,8,16,8,16]{3,2,5,4,1,0:T(8,128)(2,1)S(1)}, bf16[1,4,8,16,8,16]{3,2,5,4,1,0:T(8,128)(2,1)S(1)}, bf16[1,4,8,16,8,16]{3,2,5,4,1,0:T(8,128)(...) fusion(bf16[9,4,8,16,8,16]{3,2,5,4,1,0:T(8,128)(2,1)} %get-tupl, ...), kind=kLoop, calls=%fused_computation.267 | loop fusion | bytes 4718592 | tf_op jit(solution)/shard_map/slice | solution.py:54
  70.0 2.0 squeeze.97
  72.0 2.6 squeeze.99
  74.6 2.6 squeeze.100
  77.2 2.6 squeeze.101
  79.8 2.6 squeeze.102
  82.4 2.6 squeeze.103
  85.0 2.6 squeeze.104
  87.7 2.6 squeeze.105
  90.3 2.6 squeeze.106
  92.9 8.8 %all-gather.2 = bf16[1,512,512]{2,1,0:T(8,128)(2,1)} all-gather(bf16[1,128,512]{2,1,0:T(8,128)(2,1)} %get-tuple-element.162), channel_id=4, replica_groups=mesh['groups'=2,'rows'=4,'shard'=4] {'shard'}, dimensions={1}, use_global_device_ids=true | all-gather | bytes 655360 | tf_op jit(solution)/shard_map/all_gather | solution.py:71
  137.8 2.1 copy.447
  144.7 5.2 %collective-permute-start.2 = (bf16[1,1,128,512]{3,2,1,0:T(8,128)(2,1)}, bf16[1,1,128,512]{3,2,1,0:T(8,128)(2,1)}, u32[]{:S(2)}, u32[]{:S(2)}) collective-permute-start(bf16[1,1,128,512]{3,2,1,0:T(8,128)(2,1)} %get-tuple-element.154), channel_id=1, source_target_pairs={{0,4},{4,8},{8,12},{1,5},{5,9},{9,13},{2,6},{6,10},{10,14},{3,7},{... | collective-permute-start | bytes 393224 | tf_op jit(solution)/shard_map/ppermute | solution.py:18
  149.9 7.2 %all-gather.5 = bf16[1,512,512]{2,1,0:T(8,128)(2,1)} all-gather(bf16[1,128,512]{2,1,0:T(8,128)(2,1)S(1)} %copy-done.94), channel_id=7, replica_groups=mesh['groups'=2,'rows'=4,'shard'=4] {'shard'}, dimensions={1}, use_global_device_ids=true | all-gather | bytes 655360 | tf_op jit(solution)/shard_map/all_gather | solution.py:71
  157.1 2.6 squeeze.109
  159.7 2.6 squeeze.111
  162.3 2.6 squeeze.112
  164.9 2.6 squeeze.113
  167.5 2.6 squeeze.114
  170.1 2.8 squeeze.115
  185.2 2.7 convert_multiply_fusion
  206.9 2.0 reshape.661
  208.9 2.0 reshape.662
  222.8 5.2 %collective-permute-start.4 = (bf16[1,1,128,512]{3,2,1,0:T(8,128)(2,1)}, bf16[1,1,128,512]{3,2,1,0:T(8,128)(2,1)}, u32[]{:S(2)}, u32[]{:S(2)}) collective-permute-start(bf16[1,1,128,512]{3,2,1,0:T(8,128)(2,1)} %copy.459), channel_id=1, source_target_pairs={{0,4},{4,8},{8,12},{1,5},{5,9},{9,13},{2,6},{6,10},{10,14},{3,7},{... | collective-permute-start | bytes 393224 | tf_op jit(solution)/shard_map/ppermute | solution.py:18
  236.9 2.0 reshape.696
  240.8 2.0 reshape.698
  260.7 2.3 pad_slice_fusion
  273.1 2.0 reshape.674
  279.0 2.0 reshape.677
  294.0 5.3 %collective-permute-start.6 = (bf16[1,1,128,512]{3,2,1,0:T(8,128)(2,1)}, bf16[1,1,128,512]{3,2,1,0:T(8,128)(2,1)}, u32[]{:S(2)}, u32[]{:S(2)}) collective-permute-start(bf16[1,1,128,512]{3,2,1,0:T(8,128)(2,1)} %copy.463), channel_id=1, source_target_pairs={{0,4},{4,8},{8,12},{1,5},{5,9},{9,13},{2,6},{6,10},{10,14},{3,7},{... | collective-permute-start | bytes 393224 | tf_op jit(solution)/shard_map/ppermute | solution.py:18
  301.3 2.9 reshape.683
  306.1 2.9 reshape.685
  311.0 3.0 reshape.687
  315.8 2.9 reshape.689
  320.6 15.7 %multiply_reduce_fusion.9 = (bf16[4,16,8,16]{3,2,1,0:T(8,128)(2,1)}, bf16[4,16,8,16]{3,2,1,0:T(8,128)(2,1)}, bf16[4,16,8,16]{3,2,1,0:T(8,128)(2,1)S(1)}, bf16[4,...) fusion(f32[4,8,16,8,16]{4,3,2,1,0:T(8,128)} %reshape.690, ...), kind=kLoop, calls=%fused_computation.29 | loop fusion | flops 2211840 | bytes 5013760 | tf_op jit(solution)/shard_map/reduce_sum | solution.py:131
  343.6 2.3 convolution_convert_fusion.2
  360.8 9.3 %fusion.109 = (bf16[40,512]{1,0:T(8,128)(2,1)S(1)}, bf16[40,512]{1,0:T(8,128)(2,1)S(1)}) fusion(bf16[144,512]{1,0:T(8,128)(2,1)S(1)} %bitcast.538, bf16[144,512]{1,0:T(8,128)(2,1)} %bitcast.42), kind=kCustom, calls=%all-reduce-scatter.2 | all-reduce-scatter fusion | flops 163841 | bytes 377344
  371.6 4.3 collective-permute-start.8
  380.3 13.7 %reduce-scatter.21.cloned.1.call-done = bf16[128,512]{1,0:T(8,128)(2,1)} async-done(((bf16[512,512]{1,0:T(8,128)(2,1)}), bf16[128,512]{1,0:T(8,128)(2,1)}) %reduce-scatter.21.cloned.1.call-update) | async-done | bytes 131088
  395.8 23.0 %reduce-scatter.17.cloned.1.call-done = bf16[128,512]{1,0:T(8,128)(2,1)} async-done(((bf16[512,512]{1,0:T(8,128)(2,1)}), bf16[128,512]{1,0:T(8,128)(2,1)}) %reduce-scatter.17.cloned.1.call-update) | async-done | bytes 131088
  421.6 40.3 %all-reduce.12.cloned.1.call-done = (bf16[2,128,512]{1,2,0:T(8,128)(2,1)}, bf16[2,36,512]{2,1,0:T(8,128)(2,1)}, bf16[2,128,512]{1,2,0:T(8,128)(2,1)}) async-done(((bf16[2,128,512]{1,2,0:T(8,128)(2,1)}, bf16[2,36,512]{2,1,0:T(8,128)(2,1)}, bf16[2,128,512]{1,2,0:T(8,128)(2,1)}), (bf16[2,128,512]{1,2,0:T(8,128)(2,1)}, bf16[2,36,512]{2,1,0:T(8,128)(2,1)}, ...) | async-done | bytes 598032 | tf_op jit(solution)/shard_map/psum | solution.py:168
  (510 shorter events, 197.0 us)
Async XLA Ops:
  7.2 371.0 %reduce-scatter.23.cloned.1.call-start = ((), (), s32[]{:S(2)}) async-start(), calls=%async_computation.7 | async-start | bytes 655360
  17.5 11.0 %copy-start.108 = (bf16[2,128,512]{2,1,0:T(8,128)(2,1)S(1)}, bf16[2,128,512]{2,1,0:T(8,128)(2,1)}, u32[]{:S(2)}) copy-start(bf16[2,128,512]{2,1,0:T(8,128)(2,1)} %param.17) | copy-start | bytes 786436
  18.3 11.0 %copy-start.104 = (bf16[2,36,512]{2,0,1:T(2,128)(2,1)S(1)}, bf16[2,36,512]{2,0,1:T(2,128)(2,1)}, u32[]{:S(2)}) copy-start(bf16[2,36,512]{2,0,1:T(2,128)(2,1)} %param.16) | copy-start | bytes 221188
  20.4 16.7 %copy-start = (bf16[256,512]{1,0:T(8,128)(2,1)}, bf16[256,512]{1,0:T(8,128)(2,1)S(1)}, u32[]{:S(2)}) copy-start(bf16[256,512]{1,0:T(8,128)(2,1)S(1)} %get-tuple-element.168) | copy-start | bytes 786436
  21.1 80.6 %collective-permute-start.1 = (bf16[1,1,128,512]{3,2,1,0:T(8,128)(2,1)}, bf16[1,1,128,512]{3,2,1,0:T(8,128)(2,1)}, u32[]{:S(2)}, u32[]{:S(2)}) collective-permute-start(bf16[1,1,128,512]{3,2,1,0:T(8,128)(2,1)} %get-tuple-element.159), channel_id=1, source_target_pairs={{4,0},{8,4},{12,8},{5,1},{9,5},{13,9},{6,2},{10,6},{14,10},{7,3},{... | collective-permute-start | bytes 393224 | tf_op jit(solution)/shard_map/ppermute | solution.py:20
  22.4 79.3 %collective-permute-start = (bf16[1,1,128,512]{3,2,1,0:T(8,128)(2,1)}, bf16[1,1,128,512]{3,2,1,0:T(8,128)(2,1)}, u32[]{:S(2)}, u32[]{:S(2)}) collective-permute-start(bf16[1,1,128,512]{3,2,1,0:T(8,128)(2,1)} %get-tuple-element.158), channel_id=1, source_target_pairs={{0,4},{4,8},{8,12},{1,5},{5,9},{9,13},{2,6},{6,10},{10,14},{3,7},{... | collective-permute-start | bytes 393224 | tf_op jit(solution)/shard_map/ppermute | solution.py:18
  85.0 16.7 %copy-start.1 = (bf16[256,512]{1,0:T(8,128)(2,1)S(1)}, bf16[256,512]{1,0:T(8,128)(2,1)}, u32[]{:S(2)}) copy-start(bf16[256,512]{1,0:T(8,128)(2,1)} %copy-done) | copy-start | bytes 786436
  109.3 7.1 %copy-start.80 = (bf16[1,2,128,512]{3,2,1,0:T(8,128)(2,1)S(1)}, bf16[1,2,128,512]{3,2,1,0:T(8,128)(2,1)}, u32[]{:S(2)}) copy-start(bf16[1,2,128,512]{3,2,1,0:T(8,128)(2,1)} %get-tuple-element.129) | copy-start | bytes 786436
  119.0 14.2 %copy-start.2 = (bf16[256,4,128]{0,2,1:T(8,128)(2,1)S(1)}, bf16[256,4,128]{0,2,1:T(8,128)(2,1)}, u32[]{:S(2)}) copy-start(bf16[256,4,128]{0,2,1:T(8,128)(2,1)} %copy.370) | copy-start | bytes 786436
  141.5 8.3 %copy-start.94 = (bf16[1,128,512]{2,1,0:T(8,128)(2,1)S(1)}, bf16[1,128,512]{2,1,0:T(8,128)(2,1)}, u32[]{:S(2)}) copy-start(bf16[1,128,512]{2,1,0:T(8,128)(2,1)} %get-tuple-element.163) | copy-start | bytes 393220
  143.4 32.4 %collective-permute-start.3 = (bf16[1,1,128,512]{3,2,1,0:T(8,128)(2,1)}, bf16[1,1,128,512]{3,2,1,0:T(8,128)(2,1)}, u32[]{:S(2)}, u32[]{:S(2)}) collective-permute-start(bf16[1,1,128,512]{3,2,1,0:T(8,128)(2,1)} %get-tuple-element.155), channel_id=1, source_target_pairs={{4,0},{8,4},{12,8},{5,1},{9,5},{13,9},{6,2},{10,6},{14,10},{7,3},{... | collective-permute-start | bytes 393224 | tf_op jit(solution)/shard_map/ppermute | solution.py:20
  144.7 31.1 %collective-permute-start.2 = (bf16[1,1,128,512]{3,2,1,0:T(8,128)(2,1)}, bf16[1,1,128,512]{3,2,1,0:T(8,128)(2,1)}, u32[]{:S(2)}, u32[]{:S(2)}) collective-permute-start(bf16[1,1,128,512]{3,2,1,0:T(8,128)(2,1)} %get-tuple-element.154), channel_id=1, source_target_pairs={{0,4},{4,8},{8,12},{1,5},{5,9},{9,13},{2,6},{6,10},{10,14},{3,7},{... | collective-permute-start | bytes 393224 | tf_op jit(solution)/shard_map/ppermute | solution.py:18
  174.9 8.8 %copy-start.52 = (bf16[4,128,128]{1,2,0:T(8,128)(2,1)}, bf16[4,128,128]{1,2,0:T(8,128)(2,1)S(1)}, u32[]{:S(2)}) copy-start(bf16[4,128,128]{1,2,0:T(8,128)(2,1)S(1)} %squeeze.117) | copy-start | bytes 393220
  175.6 8.3 %copy-start.50 = (bf16[4,128,128]{1,2,0:T(8,128)(2,1)}, bf16[4,128,128]{1,2,0:T(8,128)(2,1)S(1)}, u32[]{:S(2)}) copy-start(bf16[4,128,128]{1,2,0:T(8,128)(2,1)S(1)} %squeeze.118) | copy-start | bytes 393220
  187.9 7.8 %copy-start.114 = (f32[256,512]{1,0:T(8,128)}, f32[256,512]{1,0:T(8,128)S(1)}, u32[]{:S(2)}) copy-start(f32[256,512]{1,0:T(8,128)S(1)} %get-tuple-element.132) | copy-start | bytes 1572868
  220.7 27.2 %collective-permute-start.5 = (bf16[1,1,128,512]{3,2,1,0:T(8,128)(2,1)}, bf16[1,1,128,512]{3,2,1,0:T(8,128)(2,1)}, u32[]{:S(2)}, u32[]{:S(2)}) collective-permute-start(bf16[1,1,128,512]{3,2,1,0:T(8,128)(2,1)} %copy.460), channel_id=1, source_target_pairs={{4,0},{8,4},{12,8},{5,1},{9,5},{13,9},{6,2},{10,6},{14,10},{7,3},{... | collective-permute-start | bytes 393224 | tf_op jit(solution)/shard_map/ppermute | solution.py:20
  222.0 8.5 %copy-start.66 = (f32[4,128,128]{2,1,0:T(8,128)S(1)}, f32[4,128,128]{2,1,0:T(8,128)}, u32[]{:S(2)}) copy-start(f32[4,128,128]{2,1,0:T(8,128)} %fusion.61) | copy-start | bytes 786436
  222.8 25.1 %collective-permute-start.4 = (bf16[1,1,128,512]{3,2,1,0:T(8,128)(2,1)}, bf16[1,1,128,512]{3,2,1,0:T(8,128)(2,1)}, u32[]{:S(2)}, u32[]{:S(2)}) collective-permute-start(bf16[1,1,128,512]{3,2,1,0:T(8,128)(2,1)} %copy.459), channel_id=1, source_target_pairs={{0,4},{4,8},{8,12},{1,5},{5,9},{9,13},{2,6},{6,10},{10,14},{3,7},{... | collective-permute-start | bytes 393224 | tf_op jit(solution)/shard_map/ppermute | solution.py:18
  246.7 132.6 %reduce-scatter.19.cloned.1.call-start = ((), (), s32[]{:S(2)}) async-start(), calls=%async_computation.5 | async-start | bytes 655360
  252.5 4.6 copy-start.12
  253.4 4.6 copy-start.14
  254.3 4.6 copy-start.16
  255.2 4.6 copy-start.3
  273.1 7.9 %copy-start.49 = (bf16[4,128,128]{1,2,0:T(8,128)(2,1)S(1)}, bf16[4,128,128]{1,2,0:T(8,128)(2,1)}, u32[]{:S(2)}) copy-start(bf16[4,128,128]{1,2,0:T(8,128)(2,1)} %squeeze.99) | copy-start | bytes 393220
  287.1 12.2 %copy-start.74 = (f32[4,128,128]{2,1,0:T(8,128)S(1)}, f32[4,128,128]{2,1,0:T(8,128)}, u32[]{:S(2)}) copy-start(f32[4,128,128]{2,1,0:T(8,128)} %fusion.63) | copy-start | bytes 786436
  291.0 63.8 %collective-permute-start.7 = (bf16[1,1,128,512]{3,2,1,0:T(8,128)(2,1)S(1)}, bf16[1,1,128,512]{3,2,1,0:T(8,128)(2,1)}, u32[]{:S(2)}, u32[]{:S(2)}) collective-permute-start(bf16[1,1,128,512]{3,2,1,0:T(8,128)(2,1)S(1)} %copy.464), channel_id=1, source_target_pairs={{4,0},{8,4},{12,8},{5,1},{9,5},{13,9},{6,2},{10,6},{14,10},{7,3},{... | collective-permute-start | bytes 393224 | tf_op jit(solution)/shard_map/ppermute | solution.py:20
  294.0 60.8 %collective-permute-start.6 = (bf16[1,1,128,512]{3,2,1,0:T(8,128)(2,1)}, bf16[1,1,128,512]{3,2,1,0:T(8,128)(2,1)}, u32[]{:S(2)}, u32[]{:S(2)}) collective-permute-start(bf16[1,1,128,512]{3,2,1,0:T(8,128)(2,1)} %copy.463), channel_id=1, source_target_pairs={{0,4},{4,8},{8,12},{1,5},{5,9},{9,13},{2,6},{6,10},{10,14},{3,7},{... | collective-permute-start | bytes 393224 | tf_op jit(solution)/shard_map/ppermute | solution.py:18
  336.3 4.9 %copy-start.103 = (bf16[4,16,8,16]{3,2,1,0:T(8,128)(2,1)S(1)}, bf16[4,16,8,16]{3,2,1,0:T(8,128)(2,1)}, u32[]{:S(2)}) copy-start(bf16[4,16,8,16]{3,2,1,0:T(8,128)(2,1)} %get-tuple-element.86) | copy-start | bytes 49156
  336.3 5.1 %copy-start.102 = (bf16[4,16,8,16]{3,2,1,0:T(8,128)(2,1)S(1)}, bf16[4,16,8,16]{3,2,1,0:T(8,128)(2,1)}, u32[]{:S(2)}) copy-start(bf16[4,16,8,16]{3,2,1,0:T(8,128)(2,1)} %get-tuple-element.87) | copy-start | bytes 49156
  336.3 5.3 %copy-start.101 = (bf16[4,16,8,16]{3,2,1,0:T(8,128)(2,1)S(1)}, bf16[4,16,8,16]{3,2,1,0:T(8,128)(2,1)}, u32[]{:S(2)}) copy-start(bf16[4,16,8,16]{3,2,1,0:T(8,128)(2,1)} %get-tuple-element.88) | copy-start | bytes 49156
  336.3 5.5 %copy-start.100 = (bf16[4,16,8,16]{3,2,1,0:T(8,128)(2,1)S(1)}, bf16[4,16,8,16]{3,2,1,0:T(8,128)(2,1)}, u32[]{:S(2)}) copy-start(bf16[4,16,8,16]{3,2,1,0:T(8,128)(2,1)} %get-tuple-element.89) | copy-start | bytes 49156
  336.3 5.8 %copy-start.99 = (bf16[4,16,8,16]{3,2,1,0:T(8,128)(2,1)S(1)}, bf16[4,16,8,16]{3,2,1,0:T(8,128)(2,1)}, u32[]{:S(2)}) copy-start(bf16[4,16,8,16]{3,2,1,0:T(8,128)(2,1)} %get-tuple-element.90) | copy-start | bytes 49156
  336.3 6.0 %copy-start.98 = (bf16[4,16,8,16]{3,2,1,0:T(8,128)(2,1)S(1)}, bf16[4,16,8,16]{3,2,1,0:T(8,128)(2,1)}, u32[]{:S(2)}) copy-start(bf16[4,16,8,16]{3,2,1,0:T(8,128)(2,1)} %get-tuple-element.74) | copy-start | bytes 49156
  337.7 5.0 %copy-start.97 = (bf16[4,16,8,16]{3,2,1,0:T(8,128)(2,1)S(1)}, bf16[4,16,8,16]{3,2,1,0:T(8,128)(2,1)}, u32[]{:S(2)}) copy-start(bf16[4,16,8,16]{3,2,1,0:T(8,128)(2,1)} %get-tuple-element.76) | copy-start | bytes 49156
  338.9 4.7 copy-start.106
  342.7 4.8 %copy-start.93 = (bf16[1,1,128,512]{3,2,1,0:T(8,128)(2,1)S(1)}, bf16[1,1,128,512]{3,2,1,0:T(8,128)(2,1)}, u32[]{:S(2)}) copy-start(bf16[1,1,128,512]{3,2,1,0:T(8,128)(2,1)} %copy.463) | copy-start | bytes 393220
  343.6 4.0 copy-start.90
  345.9 48.1 %reduce-scatter.21.cloned.1.call-start = ((), (), s32[]{:S(2)}) async-start(), calls=%async_computation.6 | async-start | bytes 655360
  349.3 4.3 copy-start.96
  349.6 4.3 copy-start.95
  351.4 5.4 %copy-start.88 = (f32[256,512]{1,0:T(8,128)S(1)}, f32[256,512]{1,0:T(8,128)}, u32[]{:S(2)}) copy-start(f32[256,512]{1,0:T(8,128)} %get-tuple-element.169) | copy-start | bytes 1572868
  354.2 64.6 %reduce-scatter.17.cloned.1.call-start = ((), (), s32[]{:S(2)}) async-start(), calls=%async_computation.4 | async-start | bytes 655360
  356.7 4.1 copy-start.111
  356.8 19.2 %copy-start.112 = (u32[32]{0:T(128)S(1)}, u32[32]{0:T(128)}, u32[]{:S(2)}) copy-start(u32[32]{0:T(128)} %constant.124) | copy-start | bytes 388
  358.3 62.3 %copy-start.20 = (bf16[1,512,512]{2,1,0:T(8,128)(2,1)S(1)}, bf16[1,512,512]{2,1,0:T(8,128)(2,1)}, u32[]{:S(2)}) copy-start(bf16[1,512,512]{2,1,0:T(8,128)(2,1)} %copy-done.19) | copy-start | bytes 1572868
  358.3 103.6 %all-reduce.12.cloned.1.call-start = ((), (), s32[]{:S(2)}) async-start(), calls=%async_computation.8 | async-start | bytes 1212416 | tf_op jit(solution)/shard_map/psum | solution.py:168
  370.1 7.0 %collective-permute-start.9 = (bf16[12,512]{1,0:T(8,128)(2,1)S(1)}, bf16[12,512]{1,0:T(8,128)(2,1)S(1)}, u32[]{:S(2)}, u32[]{:S(2)}) collective-permute-start(bf16[12,512]{1,0:T(8,128)(2,1)S(1)} %slice.537), channel_id=1, source_target_pairs={{0,1},{1,2},{2,3},{4,5},{5,6},{6,7},{8,9},{9,10},{10,11},{12,13},{... | collective-permute-start | bytes 36872
  371.6 5.7 %collective-permute-start.8 = (bf16[12,512]{1,0:T(8,128)(2,1)S(1)}, bf16[12,512]{1,0:T(8,128)(2,1)S(1)}, u32[]{:S(2)}, u32[]{:S(2)}) collective-permute-start(bf16[12,512]{1,0:T(8,128)(2,1)S(1)} %slice.536), channel_id=1, source_target_pairs={{0,1},{1,2},{2,3},{4,5},{5,6},{6,7},{8,9},{9,10},{10,11},{12,13},{... | collective-permute-start | bytes 36872
  (85 other events, 170.4 us)
Sparse Core Ops, SparseCore 0:
  246.8 21.4 reduce-scatter.22
  346.0 22.7 reduce-scatter.18
  371.8 22.1 reduce-scatter.20
  397.1 21.6 reduce-scatter.16
  421.8 40.0 all-reduce.11
where the time goes:
time: 482 us; the launch traced here: 473 us
  local copies, waits for them, and re-layouts  206 us (43%)
  waiting for transfers between devices  77.2 us (16%)
  blocking collectives  55.2 us (11%)
  matrix products  49.6 us (10%)
  other arithmetic  36.9 us (8%)
  starting transfers between devices  32.2 us (7%)
  between operations  16.6 us (3%)
    reshape x52, local copies, waits for them, and re-layouts, grouped_taps(): window = window.reshape(-1, kernel.shape[1], kernel.shape[2])  60.5 us
    squeeze x18, local copies, waits for them, and re-layouts, grouped_taps(): kernel[tap_index]  41.4 us
    psum x1, waiting for transfers between devices, body(): lax.psum(jnp.stack([entry[0] for entry in shares]).astype(jnp.bfloat16),...  40.3 us
    reshape x18, local copies, waits for them, and re-layouts, body(): blockwise.reshape(sections, members, group_width, members, group_width)  37.3 us
    unnamed x11, waiting for transfers between devices  36.8 us
    unnamed x273, local copies, waits for them, and re-layouts  24.9 us
    ppermute x4, starting transfers between devices, extended_2(): lax.ppermute(tail, axis, [(i, (i + 1) % count) for i in range(ends)])  20.9 us
    dot_general x36, matrix products, grouped_taps(): jnp.einsum(pattern, window, kernel[tap_index], preferred_element_type=jnp...  18.3 us
  transfers between devices with their start and end apart: 15, of which 3 were waited for; matrix products, arithmetic and copies ran while one was open for 42% of the time, Pallas kernels for 0%

commit v1 on v0

--- a/solution.py
+++ b/solution.py
@@ -5,6 +5,19 @@
 from jax.sharding import PartitionSpec as P
 
 GW = 16
+
+
+def collect(x, axis, dim):
+    ways = lax.axis_size(axis)
+    up = [(d, (d + 1) % ways) for d in range(ways)]
+    down = [(d, (d - 1) % ways) for d in range(ways)]
+    earlier, later = ([x], [x])
+    for _ in range(ways // 2):
+        earlier.append(lax.ppermute(earlier[-1], axis, up))
+    for _ in range((ways - 1) // 2):
+        later.append(lax.ppermute(later[-1], axis, down))
+    line = jnp.concatenate([*earlier[::-1], *later[1:]], axis=dim)
+    return jnp.roll(line, (lax.axis_index(axis) - ways // 2) * x.shape[dim], axis=dim)
 
 
 def extended_2(cells, sides, width):
@@ -68,7 +81,7 @@
         full_in, full_group, full_out = (
             lax.all_gather(weight_in[block_index], "shard", axis=0, tiled=True),
             lax.all_gather(weight_group[block_index], "shard", axis=0, tiled=True),
-            lax.all_gather(weight_out[block_index], "shard", axis=0, tiled=True),
+            collect(weight_out[block_index], "shard", 0),
         )
         hidden_width = full_in.shape[1]
         kernel = block_kernel(full_group, hidden_width, group_width)

time: 482 us -> 490 us (1.017)
  starting transfers between devices: 32.2 us -> 38.2 us
    ppermute x0 -> x6, starting transfers between devices: none -> 5.59 us  [the longest x2 3.83 us: collect(): later.append(lax.ppermute(later[-1], axis, down))]
    unnamed x273 -> x271, local copies, waits for them, and re-layouts: 24.9 us -> 24.9 us
  transfers between devices with their start and end apart: 15 -> 21, of which waited for: 3 -> 4; matrix products, arithmetic and copies ran while one was open for 42% -> 53% of each run, Pallas kernels for 0% -> 0%
where the time goes in v1:
time: 490 us; the launch traced here: 482 us
  local copies, waits for them, and re-layouts  206 us (42%)
  waiting for transfers between devices  78.5 us (16%)
  blocking collectives  54 us (11%)
  matrix products  51 us (10%)
  starting transfers between devices  38.2 us (8%)
  other arithmetic  36.9 us (8%)
  between operations  16.6 us (3%)
    reshape x52, local copies, waits for them, and re-layouts, grouped_taps(): window = window.reshape(-1, kernel.shape[1], kernel.shape[2])  60.8 us
    squeeze x18, local copies, waits for them, and re-layouts, grouped_taps(): kernel[tap_index]  41.2 us
    psum x1, waiting for transfers between devices, body(): lax.psum(jnp.stack([entry[0] for entry in shares]).astype(jnp.bfloat16),...  40.3 us
    reshape x18, local copies, waits for them, and re-layouts, body(): blockwise.reshape(sections, members, group_width, members, group_width)  37.3 us
    unnamed x11, waiting for transfers between devices  36.8 us
    unnamed x271, local copies, waits for them, and re-layouts  24.9 us
    ppermute x4, starting transfers between devices, extended_2(): lax.ppermute(tail, axis, [(i, (i + 1) % count) for i in range(ends)])  21.4 us
    dot_general x36, matrix products, grouped_taps(): jnp.einsum(pattern, window, kernel[tap_index], preferred_element_type=jnp...  18.3 us
  transfers between devices with their start and end apart: 21, of which 4 were waited for; matrix products, arithmetic and copies ran while one was open for 53% of the time, Pallas kernels for 0%

profile of v1, /device:TPU:0, one launch (start us, length us, event | category | flops | bytes accessed | tf_op | source)
XLA Modules:
  0.0 481.8 jit_solution(7589545823959790783)
XLA Ops:
  13.7 7.6 %all-gather.1 = bf16[1,512,512]{2,1,0:T(8,128)(2,1)S(1)} all-gather(bf16[1,128,512]{2,1,0:T(8,128)(2,1)S(1)} %get-tuple-element.165), channel_id=3, replica_groups=mesh['groups'=2,'rows'=4,'shard'=4] {'shard'}, dimensions={1}, use_global_device_ids=true | all-gather | bytes 655360 | tf_op jit(solution)/shard_map/all_gather | solution.py:82
  22.1 2.1 multiply_convert_fusion.5
  26.2 5.2 %collective-permute-start = (bf16[1,1,128,512]{3,2,1,0:T(8,128)(2,1)}, bf16[1,1,128,512]{3,2,1,0:T(8,128)(2,1)}, u32[]{:S(2)}, u32[]{:S(2)}) collective-permute-start(bf16[1,1,128,512]{3,2,1,0:T(8,128)(2,1)} %get-tuple-element.163), channel_id=1, source_target_pairs={{0,4},{4,8},{8,12},{1,5},{5,9},{9,13},{2,6},{6,10},{10,14},{3,7},{... | collective-permute-start | bytes 393224 | tf_op jit(solution)/shard_map/ppermute | solution.py:31
  32.5 6.2 %all-gather = bf16[1,144,512]{2,0,1:T(2,128)(2,1)S(1)} all-gather(bf16[1,36,512]{2,0,1:T(2,128)(2,1)S(1)} %get-tuple-element.167), channel_id=2, replica_groups=mesh['groups'=2,'rows'=4,'shard'=4] {'shard'}, dimensions={1}, use_global_device_ids=true | all-gather | bytes 184320 | tf_op jit(solution)/shard_map/all_gather | solution.py:83
  41.9 6.0 %all-gather.2 = bf16[1,144,512]{2,0,1:T(2,128)(2,1)S(1)} all-gather(bf16[1,36,512]{2,0,1:T(2,128)(2,1)S(1)} %get-tuple-element.168), channel_id=4, replica_groups=mesh['groups'=2,'rows'=4,'shard'=4] {'shard'}, dimensions={1}, use_global_device_ids=true | all-gather | bytes 184320 | tf_op jit(solution)/shard_map/all_gather | solution.py:83
  51.1 9.5 %all-gather.3 = bf16[1,512,512]{2,1,0:T(8,128)(2,1)} all-gather(bf16[1,128,512]{2,1,0:T(8,128)(2,1)} %get-tuple-element.166), channel_id=5, replica_groups=mesh['groups'=2,'rows'=4,'shard'=4] {'shard'}, dimensions={1}, use_global_device_ids=true | all-gather | bytes 655360 | tf_op jit(solution)/shard_map/all_gather | solution.py:82
  60.6 4.3 broadcast_multiply_fusion.1
  65.0 8.6 %fusion.130 = (bf16[1,4,8,16,8,16]{3,2,5,4,1,0:T(8,128)(2,1)S(1)}, bf16[1,4,8,16,8,16]{3,2,5,4,1,0:T(8,128)(2,1)S(1)}, bf16[1,4,8,16,8,16]{3,2,5,4,1,0:T(8,128)(...) fusion(bf16[9,4,8,16,8,16]{3,2,5,4,1,0:T(8,128)(2,1)} %get-tupl, ...), kind=kLoop, calls=%fused_computation.301 | loop fusion | bytes 4718592 | tf_op jit(solution)/shard_map/slice | solution.py:67
  73.5 2.0 squeeze.97
  75.6 2.6 squeeze.99
  78.2 2.6 squeeze.100
  80.8 2.6 squeeze.101
  83.4 2.6 squeeze.102
  86.0 2.6 squeeze.103
  88.6 2.6 squeeze.104
  91.2 2.6 squeeze.105
  93.8 2.6 squeeze.106
  96.4 8.3 %all-gather.4 = bf16[1,512,512]{2,1,0:T(8,128)(2,1)} all-gather(bf16[1,128,512]{2,1,0:T(8,128)(2,1)} %get-tuple-element.147), channel_id=6, replica_groups=mesh['groups'=2,'rows'=4,'shard'=4] {'shard'}, dimensions={1}, use_global_device_ids=true | all-gather | bytes 655360 | tf_op jit(solution)/shard_map/all_gather | solution.py:116
  142.7 2.0 copy.447
  146.2 2.2 convolution_add_fusion.35
  151.6 5.2 %collective-permute-start.5 = (bf16[1,1,128,512]{3,2,1,0:T(8,128)(2,1)}, bf16[1,1,128,512]{3,2,1,0:T(8,128)(2,1)}, u32[]{:S(2)}, u32[]{:S(2)}) collective-permute-start(bf16[1,1,128,512]{3,2,1,0:T(8,128)(2,1)} %get-tuple-element.159), channel_id=1, source_target_pairs={{0,4},{4,8},{8,12},{1,5},{5,9},{9,13},{2,6},{6,10},{10,14},{3,7},{... | collective-permute-start | bytes 393224 | tf_op jit(solution)/shard_map/ppermute | solution.py:31
  156.8 6.9 %all-gather.5 = bf16[1,512,512]{2,1,0:T(8,128)(2,1)} all-gather(bf16[1,128,512]{2,1,0:T(8,128)(2,1)S(1)} %copy-done.93), channel_id=7, replica_groups=mesh['groups'=2,'rows'=4,'shard'=4] {'shard'}, dimensions={1}, use_global_device_ids=true | all-gather | bytes 655360 | tf_op jit(solution)/shard_map/all_gather | solution.py:116
  163.7 2.6 squeeze.109
  166.3 2.6 squeeze.111
  168.9 2.6 squeeze.112
  171.5 2.6 squeeze.113
  174.1 2.6 squeeze.114
  176.7 2.6 squeeze.115
  192.3 3.5 convert_multiply_fusion
  208.9 2.0 reshape.658
  216.8 2.0 reshape.662
  230.3 5.4 %collective-permute-start.10 = (bf16[1,1,128,512]{3,2,1,0:T(8,128)(2,1)}, bf16[1,1,128,512]{3,2,1,0:T(8,128)(2,1)}, u32[]{:S(2)}, u32[]{:S(2)}) collective-permute-start(bf16[1,1,128,512]{3,2,1,0:T(8,128)(2,1)} %copy.459), channel_id=1, source_target_pairs={{0,4},{4,8},{8,12},{1,5},{5,9},{9,13},{2,6},{6,10},{10,14},{3,7},{... | collective-permute-start | bytes 393224 | tf_op jit(solution)/shard_map/ppermute | solution.py:31
  244.7 2.0 reshape.696
  248.6 2.0 reshape.698
  268.6 2.3 pad_slice_fusion
  281.1 2.0 reshape.674
  302.1 5.6 %collective-permute-start.12 = (bf16[1,1,128,512]{3,2,1,0:T(8,128)(2,1)}, bf16[1,1,128,512]{3,2,1,0:T(8,128)(2,1)}, u32[]{:S(2)}, u32[]{:S(2)}) collective-permute-start(bf16[1,1,128,512]{3,2,1,0:T(8,128)(2,1)} %copy.463), channel_id=1, source_target_pairs={{0,4},{4,8},{8,12},{1,5},{5,9},{9,13},{2,6},{6,10},{10,14},{3,7},{... | collective-permute-start | bytes 393224 | tf_op jit(solution)/shard_map/ppermute | solution.py:31
  309.6 2.9 reshape.683
  314.4 2.9 reshape.685
  319.3 3.0 reshape.687
  324.2 2.8 reshape.689
  328.9 15.7 %multiply_reduce_fusion.9 = (bf16[4,16,8,16]{3,2,1,0:T(8,128)(2,1)}, bf16[4,16,8,16]{3,2,1,0:T(8,128)(2,1)}, bf16[4,16,8,16]{3,2,1,0:T(8,128)(2,1)S(1)}, bf16[4,...) fusion(f32[4,8,16,8,16]{4,3,2,1,0:T(8,128)} %reshape.690, ...), kind=kLoop, calls=%fused_computation.29 | loop fusion | flops 2211840 | bytes 5013760 | tf_op jit(solution)/shard_map/reduce_sum | solution.py:144
  351.9 2.3 convolution_convert_fusion.2
  369.1 9.5 %fusion.129 = (bf16[40,512]{1,0:T(8,128)(2,1)S(1)}, bf16[40,512]{1,0:T(8,128)(2,1)S(1)}) fusion(bf16[144,512]{1,0:T(8,128)(2,1)S(1)} %bitcast.536, bf16[144,512]{1,0:T(8,128)(2,1)} %bitcast.44), kind=kCustom, calls=%all-reduce-scatter.2 | all-reduce-scatter fusion | flops 163841 | bytes 377344
  380.1 4.3 collective-permute-start.14
  388.8 13.7 %reduce-scatter.21.cloned.1.call-done = bf16[128,512]{1,0:T(8,128)(2,1)} async-done(((bf16[512,512]{1,0:T(8,128)(2,1)}), bf16[128,512]{1,0:T(8,128)(2,1)}) %reduce-scatter.21.cloned.1.call-update) | async-done | bytes 131088
  404.2 23.0 %reduce-scatter.17.cloned.1.call-done = bf16[128,512]{1,0:T(8,128)(2,1)} async-done(((bf16[512,512]{1,0:T(8,128)(2,1)}), bf16[128,512]{1,0:T(8,128)(2,1)}) %reduce-scatter.17.cloned.1.call-update) | async-done | bytes 131088
  430.1 40.3 %all-reduce.12.cloned.1.call-done = (bf16[2,128,512]{1,2,0:T(8,128)(2,1)}, bf16[2,36,512]{2,1,0:T(8,128)(2,1)}, bf16[2,128,512]{1,2,0:T(8,128)(2,1)}) async-done(((bf16[2,128,512]{1,2,0:T(8,128)(2,1)}, bf16[2,36,512]{2,1,0:T(8,128)(2,1)}, bf16[2,128,512]{1,2,0:T(8,128)(2,1)}), (bf16[2,128,512]{1,2,0:T(8,128)(2,1)}, bf16[2,36,512]{2,1,0:T(8,128)(2,1)}, ...) | async-done | bytes 598032 | tf_op jit(solution)/shard_map/psum | solution.py:181
  (520 shorter events, 205.4 us)
Async XLA Ops:
  7.2 379.5 %reduce-scatter.23.cloned.1.call-start = ((), (), s32[]{:S(2)}) async-start(), calls=%async_computation.7 | async-start | bytes 655360
  9.0 173.1 %collective-permute-start.7 = (bf16[128,512]{1,0:T(8,128)(2,1)}, bf16[128,512]{1,0:T(8,128)(2,1)}, u32[]{:S(2)}, u32[]{:S(2)}) collective-permute-start(bf16[128,512]{1,0:T(8,128)(2,1)} %get-tuple-element.146), channel_id=1, source_target_pairs={{0,1},{1,2},{2,3},{3,0},{4,5},{5,6},{6,7},{7,4},{8,9},{9,10},{10,1... | collective-permute-start | bytes 393224 | tf_op jit(solution)/shard_map/ppermute | solution.py:16
  9.4 182.8 %collective-permute-start.9 = (bf16[128,512]{1,0:T(8,128)(2,1)}, bf16[128,512]{1,0:T(8,128)(2,1)}, u32[]{:S(2)}, u32[]{:S(2)}) collective-permute-start(bf16[128,512]{1,0:T(8,128)(2,1)} %get-tuple-element.146), channel_id=1, source_target_pairs={{0,3},{1,0},{2,1},{3,2},{4,7},{5,4},{6,5},{7,6},{8,11},{9,8},{10,9... | collective-permute-start | bytes 393224 | tf_op jit(solution)/shard_map/ppermute | solution.py:18
  11.4 130.1 %collective-permute-start.2 = (bf16[128,512]{1,0:T(8,128)(2,1)}, bf16[128,512]{1,0:T(8,128)(2,1)}, u32[]{:S(2)}, u32[]{:S(2)}) collective-permute-start(bf16[128,512]{1,0:T(8,128)(2,1)} %get-tuple-element.145), channel_id=1, source_target_pairs={{0,1},{1,2},{2,3},{3,0},{4,5},{5,6},{6,7},{7,4},{8,9},{9,10},{10,1... | collective-permute-start | bytes 393224 | tf_op jit(solution)/shard_map/ppermute | solution.py:16
  22.1 10.3 %copy-start.104 = (bf16[2,36,512]{2,0,1:T(2,128)(2,1)S(1)}, bf16[2,36,512]{2,0,1:T(2,128)(2,1)}, u32[]{:S(2)}) copy-start(bf16[2,36,512]{2,0,1:T(2,128)(2,1)} %param.18) | copy-start | bytes 221188
  24.1 16.3 %copy-start = (bf16[256,512]{1,0:T(8,128)(2,1)}, bf16[256,512]{1,0:T(8,128)(2,1)S(1)}, u32[]{:S(2)}) copy-start(bf16[256,512]{1,0:T(8,128)(2,1)S(1)} %get-tuple-element.171) | copy-start | bytes 786436
  24.9 79.8 %collective-permute-start.1 = (bf16[1,1,128,512]{3,2,1,0:T(8,128)(2,1)}, bf16[1,1,128,512]{3,2,1,0:T(8,128)(2,1)}, u32[]{:S(2)}, u32[]{:S(2)}) collective-permute-start(bf16[1,1,128,512]{3,2,1,0:T(8,128)(2,1)} %get-tuple-element.164), channel_id=1, source_target_pairs={{4,0},{8,4},{12,8},{5,1},{9,5},{13,9},{6,2},{10,6},{14,10},{7,3},{... | collective-permute-start | bytes 393224 | tf_op jit(solution)/shard_map/ppermute | solution.py:33
  26.2 80.5 %collective-permute-start = (bf16[1,1,128,512]{3,2,1,0:T(8,128)(2,1)}, bf16[1,1,128,512]{3,2,1,0:T(8,128)(2,1)}, u32[]{:S(2)}, u32[]{:S(2)}) collective-permute-start(bf16[1,1,128,512]{3,2,1,0:T(8,128)(2,1)} %get-tuple-element.163), channel_id=1, source_target_pairs={{0,4},{4,8},{8,12},{1,5},{5,9},{9,13},{2,6},{6,10},{10,14},{3,7},{... | collective-permute-start | bytes 393224 | tf_op jit(solution)/shard_map/ppermute | solution.py:31
  88.6 18.1 %copy-start.1 = (bf16[256,512]{1,0:T(8,128)(2,1)S(1)}, bf16[256,512]{1,0:T(8,128)(2,1)}, u32[]{:S(2)}) copy-start(bf16[256,512]{1,0:T(8,128)(2,1)} %copy-done) | copy-start | bytes 786436
  104.8 40.0 %collective-permute-start.4 = (bf16[128,512]{1,0:T(8,128)(2,1)}, bf16[128,512]{1,0:T(8,128)(2,1)}, u32[]{:S(2)}, u32[]{:S(2)}) collective-permute-start(bf16[128,512]{1,0:T(8,128)(2,1)} %get-tuple-element.145), channel_id=1, source_target_pairs={{0,3},{1,0},{2,1},{3,2},{4,7},{5,4},{6,5},{7,6},{8,11},{9,8},{10,9... | collective-permute-start | bytes 393224 | tf_op jit(solution)/shard_map/ppermute | solution.py:18
  114.3 7.1 %copy-start.80 = (bf16[1,2,128,512]{3,2,1,0:T(8,128)(2,1)S(1)}, bf16[1,2,128,512]{3,2,1,0:T(8,128)(2,1)}, u32[]{:S(2)}) copy-start(bf16[1,2,128,512]{3,2,1,0:T(8,128)(2,1)} %get-tuple-element.130) | copy-start | bytes 786436
  124.0 14.2 %copy-start.2 = (bf16[256,4,128]{0,2,1:T(8,128)(2,1)S(1)}, bf16[256,4,128]{0,2,1:T(8,128)(2,1)}, u32[]{:S(2)}) copy-start(bf16[256,4,128]{0,2,1:T(8,128)(2,1)} %copy.370) | copy-start | bytes 786436
  141.5 4.7 collective-permute-start.3
  148.4 8.4 %copy-start.93 = (bf16[1,128,512]{2,1,0:T(8,128)(2,1)S(1)}, bf16[1,128,512]{2,1,0:T(8,128)(2,1)}, u32[]{:S(2)}) copy-start(bf16[1,128,512]{2,1,0:T(8,128)(2,1)} %get-tuple-element.144) | copy-start | bytes 393220
  150.3 32.5 %collective-permute-start.6 = (bf16[1,1,128,512]{3,2,1,0:T(8,128)(2,1)}, bf16[1,1,128,512]{3,2,1,0:T(8,128)(2,1)}, u32[]{:S(2)}, u32[]{:S(2)}) collective-permute-start(bf16[1,1,128,512]{3,2,1,0:T(8,128)(2,1)} %get-tuple-element.160), channel_id=1, source_target_pairs={{4,0},{8,4},{12,8},{5,1},{9,5},{13,9},{6,2},{10,6},{14,10},{7,3},{... | collective-permute-start | bytes 393224 | tf_op jit(solution)/shard_map/ppermute | solution.py:33
  151.6 31.2 %collective-permute-start.5 = (bf16[1,1,128,512]{3,2,1,0:T(8,128)(2,1)}, bf16[1,1,128,512]{3,2,1,0:T(8,128)(2,1)}, u32[]{:S(2)}, u32[]{:S(2)}) collective-permute-start(bf16[1,1,128,512]{3,2,1,0:T(8,128)(2,1)} %get-tuple-element.159), channel_id=1, source_target_pairs={{0,4},{4,8},{8,12},{1,5},{5,9},{9,13},{2,6},{6,10},{10,14},{3,7},{... | collective-permute-start | bytes 393224 | tf_op jit(solution)/shard_map/ppermute | solution.py:31
  181.4 9.4 %copy-start.52 = (bf16[4,128,128]{1,2,0:T(8,128)(2,1)}, bf16[4,128,128]{1,2,0:T(8,128)(2,1)S(1)}, u32[]{:S(2)}) copy-start(bf16[4,128,128]{1,2,0:T(8,128)(2,1)S(1)} %squeeze.117) | copy-start | bytes 393220
  182.1 8.9 %copy-start.50 = (bf16[4,128,128]{1,2,0:T(8,128)(2,1)}, bf16[4,128,128]{1,2,0:T(8,128)(2,1)S(1)}, u32[]{:S(2)}) copy-start(bf16[4,128,128]{1,2,0:T(8,128)(2,1)S(1)} %squeeze.118) | copy-start | bytes 393220
  182.1 10.2 %collective-permute-start.8 = (bf16[128,512]{1,0:T(8,128)(2,1)}, bf16[128,512]{1,0:T(8,128)(2,1)}, u32[]{:S(2)}, u32[]{:S(2)}) collective-permute-start(bf16[128,512]{1,0:T(8,128)(2,1)} %collective-permute-done.7), channel_id=1, source_target_pairs={{0,1},{1,2},{2,3},{3,0},{4,5},{5,6},{6,7},{7,4},{8,9},{9,10},{10,1... | collective-permute-start | bytes 393224 | tf_op jit(solution)/shard_map/ppermute | solution.py:16
  195.7 7.9 %copy-start.113 = (f32[256,512]{1,0:T(8,128)}, f32[256,512]{1,0:T(8,128)S(1)}, u32[]{:S(2)}) copy-start(f32[256,512]{1,0:T(8,128)S(1)} %get-tuple-element.133) | copy-start | bytes 1572868
  228.2 27.5 %collective-permute-start.11 = (bf16[1,1,128,512]{3,2,1,0:T(8,128)(2,1)}, bf16[1,1,128,512]{3,2,1,0:T(8,128)(2,1)}, u32[]{:S(2)}, u32[]{:S(2)}) collective-permute-start(bf16[1,1,128,512]{3,2,1,0:T(8,128)(2,1)} %copy.460), channel_id=1, source_target_pairs={{4,0},{8,4},{12,8},{5,1},{9,5},{13,9},{6,2},{10,6},{14,10},{7,3},{... | collective-permute-start | bytes 393224 | tf_op jit(solution)/shard_map/ppermute | solution.py:33
  229.5 8.8 %copy-start.66 = (f32[4,128,128]{2,1,0:T(8,128)S(1)}, f32[4,128,128]{2,1,0:T(8,128)}, u32[]{:S(2)}) copy-start(f32[4,128,128]{2,1,0:T(8,128)} %fusion.77) | copy-start | bytes 786436
  230.3 25.4 %collective-permute-start.10 = (bf16[1,1,128,512]{3,2,1,0:T(8,128)(2,1)}, bf16[1,1,128,512]{3,2,1,0:T(8,128)(2,1)}, u32[]{:S(2)}, u32[]{:S(2)}) collective-permute-start(bf16[1,1,128,512]{3,2,1,0:T(8,128)(2,1)} %copy.459), channel_id=1, source_target_pairs={{0,4},{4,8},{8,12},{1,5},{5,9},{9,13},{2,6},{6,10},{10,14},{3,7},{... | collective-permute-start | bytes 393224 | tf_op jit(solution)/shard_map/ppermute | solution.py:31
  254.5 133.2 %reduce-scatter.19.cloned.1.call-start = ((), (), s32[]{:S(2)}) async-start(), calls=%async_computation.5 | async-start | bytes 655360
  260.3 4.6 copy-start.12
  261.3 4.6 copy-start.14
  263.1 4.6 copy-start.3
  281.1 7.9 %copy-start.49 = (bf16[4,128,128]{1,2,0:T(8,128)(2,1)S(1)}, bf16[4,128,128]{1,2,0:T(8,128)(2,1)}, u32[]{:S(2)}) copy-start(bf16[4,128,128]{1,2,0:T(8,128)(2,1)} %squeeze.99) | copy-start | bytes 393220
  295.2 12.5 %copy-start.74 = (f32[4,128,128]{2,1,0:T(8,128)S(1)}, f32[4,128,128]{2,1,0:T(8,128)}, u32[]{:S(2)}) copy-start(f32[4,128,128]{2,1,0:T(8,128)} %fusion.79) | copy-start | bytes 786436
  299.0 64.0 %collective-permute-start.13 = (bf16[1,1,128,512]{3,2,1,0:T(8,128)(2,1)S(1)}, bf16[1,1,128,512]{3,2,1,0:T(8,128)(2,1)}, u32[]{:S(2)}, u32[]{:S(2)}) collective-permute-start(bf16[1,1,128,512]{3,2,1,0:T(8,128)(2,1)S(1)} %copy.464), channel_id=1, source_target_pairs={{4,0},{8,4},{12,8},{5,1},{9,5},{13,9},{6,2},{10,6},{14,10},{7,3},{... | collective-permute-start | bytes 393224 | tf_op jit(solution)/shard_map/ppermute | solution.py:33
  302.1 61.0 %collective-permute-start.12 = (bf16[1,1,128,512]{3,2,1,0:T(8,128)(2,1)}, bf16[1,1,128,512]{3,2,1,0:T(8,128)(2,1)}, u32[]{:S(2)}, u32[]{:S(2)}) collective-permute-start(bf16[1,1,128,512]{3,2,1,0:T(8,128)(2,1)} %copy.463), channel_id=1, source_target_pairs={{0,4},{4,8},{8,12},{1,5},{5,9},{9,13},{2,6},{6,10},{10,14},{3,7},{... | collective-permute-start | bytes 393224 | tf_op jit(solution)/shard_map/ppermute | solution.py:31
  344.6 4.9 %copy-start.103 = (bf16[4,16,8,16]{3,2,1,0:T(8,128)(2,1)S(1)}, bf16[4,16,8,16]{3,2,1,0:T(8,128)(2,1)}, u32[]{:S(2)}) copy-start(bf16[4,16,8,16]{3,2,1,0:T(8,128)(2,1)} %get-tuple-element.87) | copy-start | bytes 49156
  344.6 5.1 %copy-start.102 = (bf16[4,16,8,16]{3,2,1,0:T(8,128)(2,1)S(1)}, bf16[4,16,8,16]{3,2,1,0:T(8,128)(2,1)}, u32[]{:S(2)}) copy-start(bf16[4,16,8,16]{3,2,1,0:T(8,128)(2,1)} %get-tuple-element.88) | copy-start | bytes 49156
  344.6 5.3 %copy-start.101 = (bf16[4,16,8,16]{3,2,1,0:T(8,128)(2,1)S(1)}, bf16[4,16,8,16]{3,2,1,0:T(8,128)(2,1)}, u32[]{:S(2)}) copy-start(bf16[4,16,8,16]{3,2,1,0:T(8,128)(2,1)} %get-tuple-element.89) | copy-start | bytes 49156
  344.6 5.5 %copy-start.100 = (bf16[4,16,8,16]{3,2,1,0:T(8,128)(2,1)S(1)}, bf16[4,16,8,16]{3,2,1,0:T(8,128)(2,1)}, u32[]{:S(2)}) copy-start(bf16[4,16,8,16]{3,2,1,0:T(8,128)(2,1)} %get-tuple-element.90) | copy-start | bytes 49156
  344.6 5.8 %copy-start.99 = (bf16[4,16,8,16]{3,2,1,0:T(8,128)(2,1)S(1)}, bf16[4,16,8,16]{3,2,1,0:T(8,128)(2,1)}, u32[]{:S(2)}) copy-start(bf16[4,16,8,16]{3,2,1,0:T(8,128)(2,1)} %get-tuple-element.91) | copy-start | bytes 49156
  344.6 6.0 %copy-start.98 = (bf16[4,16,8,16]{3,2,1,0:T(8,128)(2,1)S(1)}, bf16[4,16,8,16]{3,2,1,0:T(8,128)(2,1)}, u32[]{:S(2)}) copy-start(bf16[4,16,8,16]{3,2,1,0:T(8,128)(2,1)} %get-tuple-element.75) | copy-start | bytes 49156
  346.0 5.0 %copy-start.97 = (bf16[4,16,8,16]{3,2,1,0:T(8,128)(2,1)S(1)}, bf16[4,16,8,16]{3,2,1,0:T(8,128)(2,1)}, u32[]{:S(2)}) copy-start(bf16[4,16,8,16]{3,2,1,0:T(8,128)(2,1)} %get-tuple-element.77) | copy-start | bytes 49156
  347.2 4.7 copy-start.106
  351.0 4.7 copy-start.94
  354.2 48.3 %reduce-scatter.21.cloned.1.call-start = ((), (), s32[]{:S(2)}) async-start(), calls=%async_computation.6 | async-start | bytes 655360
  359.6 5.4 %copy-start.88 = (f32[256,512]{1,0:T(8,128)S(1)}, f32[256,512]{1,0:T(8,128)}, u32[]{:S(2)}) copy-start(f32[256,512]{1,0:T(8,128)} %get-tuple-element.172) | copy-start | bytes 1572868
  362.4 64.8 %reduce-scatter.17.cloned.1.call-start = ((), (), s32[]{:S(2)}) async-start(), calls=%async_computation.4 | async-start | bytes 655360
  365.0 19.3 %copy-start.111 = (u32[32]{0:T(128)S(1)}, u32[32]{0:T(128)}, u32[]{:S(2)}) copy-start(u32[32]{0:T(128)} %constant.150) | copy-start | bytes 388
  366.6 62.5 %copy-start.20 = (bf16[1,512,512]{2,1,0:T(8,128)(2,1)S(1)}, bf16[1,512,512]{2,1,0:T(8,128)(2,1)}, u32[]{:S(2)}) copy-start(bf16[1,512,512]{2,1,0:T(8,128)(2,1)} %copy-done.19) | copy-start | bytes 1572868
  366.6 103.8 %all-reduce.12.cloned.1.call-start = ((), (), s32[]{:S(2)}) async-start(), calls=%async_computation.8 | async-start | bytes 1212416 | tf_op jit(solution)/shard_map/psum | solution.py:181
  378.6 7.0 %collective-permute-start.15 = (bf16[12,512]{1,0:T(8,128)(2,1)S(1)}, bf16[12,512]{1,0:T(8,128)(2,1)S(1)}, u32[]{:S(2)}, u32[]{:S(2)}) collective-permute-start(bf16[12,512]{1,0:T(8,128)(2,1)S(1)} %slice.537), channel_id=1, source_target_pairs={{0,1},{1,2},{2,3},{4,5},{5,6},{6,7},{8,9},{9,10},{10,11},{12,13},{... | collective-permute-start | bytes 36872
  380.1 5.7 %collective-permute-start.14 = (bf16[12,512]{1,0:T(8,128)(2,1)S(1)}, bf16[12,512]{1,0:T(8,128)(2,1)S(1)}, u32[]{:S(2)}, u32[]{:S(2)}) collective-permute-start(bf16[12,512]{1,0:T(8,128)(2,1)S(1)} %slice.536), channel_id=1, source_target_pairs={{0,1},{1,2},{2,3},{4,5},{5,6},{6,7},{8,9},{9,10},{10,11},{12,13},{... | collective-permute-start | bytes 36872
  (90 other events, 195.5 us)
Sparse Core Ops, SparseCore 0:
  254.6 21.6 reduce-scatter.22
  354.3 22.7 reduce-scatter.18
  380.2 22.1 reduce-scatter.20
  405.5 21.6 reduce-scatter.16
  430.2 40.1 all-reduce.11
